TPU v7x, 256 devices: a whole 4x4x8 slice. The times are simulated.
256 devices in a mesh: rows: 8 (over z_lo, core), cols: 32 (over y, x, z_hi).
Axes of the slice: x: 4, y: 4, z: 8 (z_hi: 2, z_lo: 4; z = z_hi * 4 + z_lo), core: 2. Of those that a mesh axis runs over, the one named last changes fastest.
Arguments:
- orbitals: bfloat16 [32768, 16384], P('rows', 'cols'), may hold values from -0.4453125 to 0.4453125
- applied: bfloat16 [32768, 16384], P('rows', 'cols'), may hold values from -0.4453125 to 0.4453125
Outputs:
- gram_blocks: float32 [3, 16384, 512], P(None, 'cols')
- ham_blocks: float32 [3, 16384, 512], P(None, 'cols')
All inputs are finite; a program needn't handle non-finite values.
Results may differ from a plain program's by a relative error of at most 0.0003.
Values may be sent and summed in bfloat16 or wider, within the bound.
A program may use at most 128 MiB of HBM per device.

v0:
```python
import jax
import jax.numpy as jnp
from jax import lax
from jax.sharding import PartitionSpec as P

ROUNDS = 2


def from_behind(block, axis, distance):
    devices = range(lax.axis_size(axis))
    route = [((i - distance) % len(devices), i) for i in devices]
    return lax.ppermute(block, axis, route)


def block_pair(own, own_applied, other):
    gram = jnp.dot(own.T, other, preferred_element_type=jnp.float32)
    ham = jnp.dot(other.T, own_applied, preferred_element_type=jnp.float32)
    return (gram, ham)


def per_device(orbitals, applied):
    gram_list = []
    ham_list = []
    first_gram, first_ham = block_pair(orbitals, applied, orbitals)
    gram_list.append(first_gram)
    ham_list.append(first_ham)
    held = orbitals
    for step in range(1, ROUNDS + 1):
        held = from_behind(held, "cols", 1)
        part_gram, part_ham = block_pair(orbitals, applied, held)
        gram_list.append(part_gram)
        ham_list.append(part_ham)
    gram = jnp.stack(gram_list)
    ham = jnp.stack(ham_list)
    gram, ham = lax.psum((gram, ham), "rows")
    return (gram, ham)


def solution(mesh):
    placed = (P("rows", "cols"), P("rows", "cols"))
    return jax.shard_map(
        per_device,
        mesh=mesh,
        in_specs=placed,
        out_specs=(P(None, "cols", None), P(None, "cols", None)),
        check_vma=False,
    )
```

profile of v0, /device:TPU:1, one launch (start us, length us, event | category | flops | bytes accessed | tf_op | source)
XLA Modules:
  0.0 553.9 jit_solution(9434442067762198958)
XLA Ops:
  7.2 0.0 all-reduce.3.cloned.1.call-start
  7.2 0.0 copy-start
  7.2 0.0 copy-start.1
  7.2 7.8 %collective-permute-start = (bf16[4096,512]{1,0:T(8,128)(2,1)}, bf16[4096,512]{1,0:T(8,128)(2,1)S(1)}, u32[]{:S(2)}, u32[]{:S(2)}) collective-permute-start(bf16[4096,512]{1,0:T(8,128)(2,1)} %param.2), channel_id=1, source_target_pairs={{31,0},{0,1},{1,2},{2,3},{3,4},{4,5},{5,6},{6,7},{7,8},{8,9},{9,10... | collective-permute-start | bytes 12582920 | tf_op jit(solution)/shard_map/ppermute | solution.py:12
  15.0 157.5 %collective-permute-done = bf16[4096,512]{1,0:T(8,128)(2,1)S(1)} collective-permute-done((bf16[4096,512]{1,0:T(8,128)(2,1)}, bf16[4096,512]{1,0:T(8,128)(2,1)S(1)}, u32[]{:S(2)}, u32[]{:S(2)}) %collective-permute-start) | collective-permute-done | bytes 4194336 | tf_op jit(solution)/shard_map/ppermute | solution.py:12
  172.5 0.0 collective-permute-start.1
  172.5 5.8 %convolution_bitcast_fusion.5 = f32[1,512,512]{2,1,0:T(8,128)S(1)} fusion(bf16[4096,512]{1,0:T(8,128)(2,1)} %param.2), kind=kOutput, calls=%fused_computation.7 | convolution fusion | flops 2147483648 | bytes 5242880 | tf_op jit(solution)/shard_map/dot_general | solution.py:16
  178.3 0.0 copy-done
  178.3 0.0 copy-done.1
  178.4 2.3 convolution_bitcast_fusion.2
  180.7 2.3 convolution_bitcast_fusion.1
  183.1 2.4 convolution_bitcast_fusion.4
  185.4 201.0 %collective-permute-done.1 = bf16[4096,512]{1,0:T(8,128)(2,1)S(1)} collective-permute-done((bf16[4096,512]{1,0:T(8,128)(2,1)S(1)}, bf16[4096,512]{1,0:T(8,128)(2,1)S(1)}, u32[]{:S(2)}, u32[]{:S(2)}) %collective-permute-start.1) | collective-permute-done | bytes 4194336 | tf_op jit(solution)/shard_map/ppermute | solution.py:12
  386.4 2.3 convolution_bitcast_fusion
  388.8 2.3 convolution_bitcast_fusion.3
  391.1 3.4 pad_maximum_fusion
  394.5 0.0 all-reduce.3.cloned.1.call-update
  394.5 146.9 %all-reduce.3.cloned.1.call-done = (f32[3,512,512]{2,1,0:T(8,128)}, f32[3,512,512]{2,1,0:T(8,128)}) async-done(((f32[3,512,512]{2,1,0:T(8,128)}, f32[3,512,512]{2,1,0:T(8,128)}), (f32[3,512,512]{2,1,0:T(8,128)}, f32[3,512,512]{2,1,0:T(8,128)})) %all-reduce.3.cloned.1.call-update) | async-done | bytes 6291472 | tf_op jit(solution)/shard_map/psum | solution.py:35
  541.4 0.0 copy-start.2
  541.4 4.0 copy.6
  545.4 0.0 copy-done.2
  545.4 1.7 copy.7
Async XLA Ops:
  7.2 534.2 %all-reduce.3.cloned.1.call-start = ((), (), s32[]{:S(2)}) async-start(), calls=%async_computation | async-start | bytes 12582912 | tf_op jit(solution)/shard_map/psum | solution.py:35
  7.2 171.1 %copy-start = (bf16[4096,512]{1,0:T(8,128)(2,1)S(1)}, bf16[4096,512]{1,0:T(8,128)(2,1)}, u32[]{:S(2)}) copy-start(bf16[4096,512]{1,0:T(8,128)(2,1)} %param.2) | copy-start | bytes 12582916
  7.2 171.1 %copy-start.1 = (bf16[4096,512]{1,0:T(8,128)(2,1)S(1)}, bf16[4096,512]{1,0:T(8,128)(2,1)}, u32[]{:S(2)}) copy-start(bf16[4096,512]{1,0:T(8,128)(2,1)} %param.3) | copy-start | bytes 12582916
  7.2 165.3 %collective-permute-start = (bf16[4096,512]{1,0:T(8,128)(2,1)}, bf16[4096,512]{1,0:T(8,128)(2,1)S(1)}, u32[]{:S(2)}, u32[]{:S(2)}) collective-permute-start(bf16[4096,512]{1,0:T(8,128)(2,1)} %param.2), channel_id=1, source_target_pairs={{31,0},{0,1},{1,2},{2,3},{3,4},{4,5},{5,6},{6,7},{7,8},{8,9},{9,10... | collective-permute-start | bytes 12582920 | tf_op jit(solution)/shard_map/ppermute | solution.py:12
  172.5 213.9 %collective-permute-start.1 = (bf16[4096,512]{1,0:T(8,128)(2,1)S(1)}, bf16[4096,512]{1,0:T(8,128)(2,1)S(1)}, u32[]{:S(2)}, u32[]{:S(2)}) collective-permute-start(bf16[4096,512]{1,0:T(8,128)(2,1)S(1)} %collective-permute-done), channel_id=1, source_target_pairs={{31,0},{0,1},{1,2},{2,3},{3,4},{4,5},{5,6},{6,7},{7,8},{8,9},{9,10... | collective-permute-start | bytes 12582920 | tf_op jit(solution)/shard_map/ppermute | solution.py:12
  541.4 4.0 copy-start.2
Sparse Core Ops, SparseCore 0:
  394.7 146.6 all-reduce.2
where the time goes:
time: 555 us; the launch traced here: 554 us
  waiting for transfers between devices  505 us (91%)
  matrix products  17.5 us (3%)
  between operations  14.1 us (3%)
  starting transfers between devices  7.86 us (1%)
  local copies, waits for them, and re-layouts  5.7 us (1%)
    ppermute x2, waiting for transfers between devices, from_behind(): return lax.ppermute(block, axis, route)  358 us
    psum x1, waiting for transfers between devices, per_device(): gram, ham = lax.psum((gram, ham), 'rows')  147 us
  transfers between devices with their start and end apart: 3, of which 3 were waited for; matrix products, arithmetic and copies ran while one was open for 2% of the time, Pallas kernels for 0%

commit v1 on v0

v1 whole, which is shorter than its diff:
```python
import functools

import jax
import jax.numpy as jnp
from jax import lax
from jax.experimental import pallas as pl
from jax.experimental.pallas import tpu as pltpu
from jax.sharding import PartitionSpec as P

BLOCK = 512
GRID_ROWS = 4096
STRIP = 128
CHUNKS = BLOCK // STRIP
PIECE = 512
PER_CHUNK = GRID_ROWS // PIECE
PIECES = CHUNKS * PER_CHUNK
ROUND_OF = (0, 2, 1)
UNITS = 3 * CHUNKS
AHEAD = 3
LAG = AHEAD + 2
KTILE = 512
ROWS_AT_ONCE = 16
MESH = pl.DeviceIdType.MESH


def plan():
    ready = {}
    for j in range(CHUNKS):
        ready[j] = j
        ready[CHUNKS + j] = 4 * j + 7
        ready[2 * CHUNKS + j] = PER_CHUNK * (j + 1) + AHEAD + 1
    stages = []
    for unit, at in ready.items():
        for stage, delay in enumerate((0, 1, 1 + LAG, 1 + 2 * LAG, 1 + 3 * LAG)):
            stages.append((at + delay, stage, unit))
    return sorted(stages)


def kernel(n_cols, x_ref, hx_ref, out_ref, blocks, both, part, sib_in, snd, rcv, fin,
           load_sem, r1_send, r1_recv, r2_send, r2_recv, sib_send, sib_recv,
           z_send, z_recv, fin_send, fin_recv, out_sem):
    row = lax.axis_index("rows")
    col = lax.axis_index("cols")
    core = lax.rem(row, 2)
    z = row // 2
    upper = lax.rem(col, 2)
    edge = jnp.logical_or(z == 0, z == 3)
    inner = jnp.logical_or(z == 1, z == 2)
    sibling = (row + 1 - 2 * core, col)
    beside = (row + 2 - 4 * lax.rem(z, 2), col)
    across = ((3 - z) * 2 + core, col)
    half = (row, col + 1 - 2 * upper)
    ahead = (row, lax.rem(col + 2, n_cols))
    behind = (row, lax.rem(col + n_cols - 2, n_cols))

    loads = []
    for j in range(CHUNKS):
        loads.append(pltpu.make_async_copy(
            x_ref.at[:, pl.ds(j * STRIP, STRIP)], blocks.at[j], load_sem.at[j]))
    loads.append(pltpu.make_async_copy(x_ref, both.at[:, pl.ds(0, BLOCK)], load_sem.at[CHUNKS]))
    loads.append(pltpu.make_async_copy(hx_ref, both.at[:, pl.ds(BLOCK, BLOCK)], load_sem.at[CHUNKS + 1]))
    for load in loads:
        load.start()

    barrier = pltpu.get_barrier_semaphore()
    for device in (sibling, beside, across, half, ahead, behind):
        pl.semaphore_signal(barrier, inc=1, device_id=device, device_id_type=MESH)
    pl.semaphore_wait(barrier, 6)

    def piece(slot, p):
        return blocks.at[slot + p // PER_CHUNK, pl.ds((p % PER_CHUNK) * PIECE, PIECE)]

    def remote(src, dst, send, recv, device):
        return pltpu.make_async_remote_copy(
            src_ref=src, dst_ref=dst, send_sem=send, recv_sem=recv,
            device_id=device, device_id_type=MESH)

    def two_back(p):
        return remote(piece(0, p), piece(CHUNKS, p), r2_send.at[p], r2_recv.at[p], ahead)

    def one_back(p):
        return remote(piece(upper * CHUNKS, p), piece(2 * CHUNKS, p), r1_send.at[p], r1_recv.at[p], half)

    def to_sibling(u):
        return remote(part.at[u, 1 - core], sib_in.at[u], sib_send.at[u], sib_recv.at[u], sibling)

    def edge_to_inner(u):
        return remote(snd.at[0, u], rcv.at[0, u], z_send.at[0, u], z_recv.at[0, u], beside)

    def inner_to_inner(u):
        return remote(snd.at[0, u], rcv.at[1, u], z_send.at[0, u], z_recv.at[1, u], across)

    def inner_to_edge(u):
        return remote(snd.at[1, u], rcv.at[0, u], z_send.at[1, u], z_recv.at[0, u], beside)

    def place(u):
        return out_ref.at[core, ROUND_OF[u // CHUNKS], pl.ds((u % CHUNKS) * STRIP, STRIP)]

    def fin_to_sibling(u):
        return remote(fin.at[u], place(u), fin_send.at[u], fin_recv.at[u], sibling)

    def fin_to_out(u):
        return pltpu.make_async_copy(fin.at[u], place(u), out_sem.at[u])

    def by_rows(body):
        @pl.loop(0, STRIP // ROWS_AT_ONCE)
        def _(i):
            body(pl.ds(pl.multiple_of(i * ROWS_AT_ONCE, ROWS_AT_ONCE), ROWS_AT_ONCE))

    loaded, got_two, got_one = set(), set(), set()

    def wait_load(i):
        if i not in loaded:
            loaded.add(i)
            loads[i].wait()

    def wait_two(p):
        if p not in got_two:
            got_two.add(p)
            two_back(p).wait_recv()

    def wait_one(p):
        if p not in got_one:
            got_one.add(p)
            one_back(p).wait_recv()

    def multiply(u):
        j = u % CHUNKS
        if u < CHUNKS:
            wait_load(u)
        else:
            for p in range(j * PER_CHUNK, (j + 1) * PER_CHUNK):
                (wait_two if u < 2 * CHUNKS else wait_one)(p)
        part[u] = jnp.zeros((2, STRIP, BLOCK), jnp.float32)

        @pl.loop(0, GRID_ROWS // KTILE)
        def _(k):
            ks = pl.ds(pl.multiple_of(k * KTILE, KTILE), KTILE)
            got = lax.dot_general(
                blocks[u, ks, :], both[ks, :], (((0,), (0,)), ((), ())),
                preferred_element_type=jnp.float32)
            part[u, 0] += got[:, :BLOCK]
            part[u, 1] += got[:, BLOCK:]

        to_sibling(u).start()

    def chip_sum(u):
        to_sibling(u).wait_recv()

        @pl.when(edge)
        def _():
            def body(rows):
                snd[0, u, rows, :] = part[u, core, rows, :] + sib_in[u, rows, :]
            by_rows(body)
            edge_to_inner(u).start()

    def pair_sum(u):
        @pl.when(inner)
        def _():
            edge_to_inner(u).wait_recv()

            def body(rows):
                snd[0, u, rows, :] = part[u, core, rows, :] + sib_in[u, rows, :] + rcv[0, u, rows, :]
            by_rows(body)
            inner_to_inner(u).start()

    def whole_sum(u):
        @pl.when(inner)
        def _():
            inner_to_inner(u).wait_recv()

            def body(rows):
                total = snd[0, u, rows, :] + rcv[1, u, rows, :]
                snd[1, u, rows, :] = total
                fin[u, rows, :] = total
            by_rows(body)
            inner_to_edge(u).start()
            fin_to_sibling(u).start()
            fin_to_out(u).start()

    def edge_result(u):
        @pl.when(edge)
        def _():
            inner_to_edge(u).wait_recv()

            def body(rows):
                fin[u, rows, :] = rcv[0, u, rows, :]
            by_rows(body)
            fin_to_sibling(u).start()
            fin_to_out(u).start()

    stage_of = (multiply, chip_sum, pair_sum, whole_sum, edge_result)
    todo = plan()
    sent_two = 0
    for p in range(PIECES):
        while sent_two < min(PIECES, 2 * p + 6):
            wait_load(sent_two // PER_CHUNK)
            two_back(sent_two).start()
            sent_two += 1
        wait_two(p)
        if p >= AHEAD:
            one_back(p - AHEAD).wait_send()
        one_back(p).start()
        wait_load(CHUNKS)
        wait_load(CHUNKS + 1)
        while todo and todo[0][0] <= p:
            _, stage, unit = todo.pop(0)
            stage_of[stage](unit)
    for _, stage, unit in todo:
        stage_of[stage](unit)

    for p in range(PIECES - AHEAD, PIECES):
        one_back(p).wait_send()
    for p in range(PIECES):
        two_back(p).wait_send()
    for u in range(UNITS):
        to_sibling(u).wait_send()
        fin_to_out(u).wait()
        fin_to_sibling(u).wait()

    @pl.when(edge)
    def _():
        for u in range(UNITS):
            edge_to_inner(u).wait_send()

    @pl.when(inner)
    def _():
        for u in range(UNITS):
            inner_to_inner(u).wait_send()
            inner_to_edge(u).wait_send()


def per_device(n_cols, orbitals, applied):
    f32, bf16 = jnp.float32, jnp.bfloat16
    dma = pltpu.SemaphoreType.DMA
    out = pl.pallas_call(
        functools.partial(kernel, n_cols),
        out_shape=jax.ShapeDtypeStruct((2, 3, BLOCK, BLOCK), f32),
        in_specs=[pl.BlockSpec(memory_space=pl.ANY)] * 2,
        out_specs=pl.BlockSpec(memory_space=pl.ANY),
        scratch_shapes=[
            pltpu.VMEM((3 * CHUNKS, GRID_ROWS, STRIP), bf16),
            pltpu.VMEM((GRID_ROWS, 2 * BLOCK), bf16),
            pltpu.VMEM((UNITS, 2, STRIP, BLOCK), f32),
            pltpu.VMEM((UNITS, STRIP, BLOCK), f32),
            pltpu.VMEM((2, UNITS, STRIP, BLOCK), f32),
            pltpu.VMEM((2, UNITS, STRIP, BLOCK), f32),
            pltpu.VMEM((UNITS, STRIP, BLOCK), f32),
            dma((CHUNKS + 2,)),
            dma((PIECES,)), dma((PIECES,)), dma((PIECES,)), dma((PIECES,)),
            dma((UNITS,)), dma((UNITS,)),
            dma((2, UNITS)), dma((2, UNITS)),
            dma((UNITS,)), dma((UNITS,)), dma((UNITS,)),
        ],
        compiler_params=pltpu.CompilerParams(
            collective_id=0, has_side_effects=True, vmem_limit_bytes=58 * 2**20),
    )(orbitals, applied)
    return jnp.swapaxes(out[0], 1, 2), out[1]


def solution(mesh):
    placed = (P("rows", "cols"), P("rows", "cols"))
    return jax.shard_map(
        functools.partial(per_device, mesh.shape["cols"]),
        mesh=mesh,
        in_specs=placed,
        out_specs=(P(None, "cols", None), P(None, "cols", None)),
        check_vma=False,
    )
```

time: 555 us -> 306 us (0.55)
  waiting for transfers between devices: 505 us -> 0 us
  Pallas kernels: 0 us -> 297 us
  matrix products: 17.5 us -> 0 us
  between operations: 14.1 us -> 0.64 us
  starting transfers between devices: 7.86 us -> 0 us
    ppermute x2 -> x0, waiting for transfers between devices: 358 us -> none  [from_behind(): return lax.ppermute(block, axis, route)]
    pallas_call x0 -> x1, Pallas kernels: none -> 297 us  [per_device(): pl.pallas_call(functools.partial(kernel, n_cols), out_shape=jax.ShapeDtyp...]
    psum x1 -> x0, waiting for transfers between devices: 147 us -> none  [per_device(): gram, ham = lax.psum((gram, ham), 'rows')]
    dot_general x6 -> x0, matrix products: 17.5 us -> none  [the longest x3 10.5 us: block_pair(): gram = jnp.dot(own.T, other, preferred_element_type=jnp.float32)]
    ppermute x2 -> x0, starting transfers between devices: 7.82 us -> none  [from_behind(): return lax.ppermute(block, axis, route)]
    squeeze x0 -> x1, local copies, waits for them, and re-layouts: none -> 5.57 us  [per_device(): return (jnp.swapaxes(out[0], 1, 2), out[1])]
  transfers between devices with their start and end apart: 3 -> 0, of which waited for: 3 -> 0; matrix products, arithmetic and copies ran while one was open for 2% -> 0% of each run, Pallas kernels for 0% -> 0%
where the time goes in v1:
time: 306 us
  Pallas kernels  297 us (97%)
  local copies, waits for them, and re-layouts  7.92 us (3%)
    pallas_call x1, Pallas kernels, per_device(): pl.pallas_call(functools.partial(kernel, n_cols), out_shape=jax.ShapeDtyp...  297 us

profile of v1, /device:TPU:1, one launch (start us, length us, event | category | flops | bytes accessed | tf_op | source)
XLA Modules:
  0.0 305.7 jit_solution(8283971987265334556)
XLA Ops:
  0.6 297.2 %shard_map.41 = f32[2,3,512,512]{3,2,1,0:T(8,128)} custom-call(bf16[4096,512]{1,0:T(8,128)(2,1)} %x_ref.1, bf16[4096,512]{1,0:T(8,128)(2,1)} %hx_ref.1), custom_call_target="tpu_custom_call" | custom-call | tf_op jit(solution)/shard_map/pallas_call | solution.py:236
  297.8 5.6 %slice_bitcast_fusion = (f32[3,512,512]{2,1,0:T(8,128)}, f32[3,512,512]{1,2,0:T(8,128)S(1)}) fusion(f32[2,3,512,512]{3,2,1,0:T(8,128)} %shard_map.41), kind=kLoop, calls=%fused_computation | loop fusion | bytes 12582912 | tf_op jit(solution)/shard_map/squeeze | solution.py:258
  303.4 2.4 copy.4

commit v2 on v0

v2 whole, which is shorter than its diff:
```python
import functools

import jax
import jax.numpy as jnp
from jax import lax
from jax.experimental import pallas as pl
from jax.experimental.pallas import tpu as pltpu
from jax.sharding import PartitionSpec as P

BLOCK = 512
GRID_ROWS = 4096
STRIP = 128
CHUNKS = BLOCK // STRIP
PIECE = 512
PER_CHUNK = GRID_ROWS // PIECE
PIECES = CHUNKS * PER_CHUNK
ROUND_OF = (0, 2, 1)
UNITS = 3 * CHUNKS
LAST = UNITS - 1
HALVES = 2
AHEAD = 4
DIRECT = 4
LEAD = 6
SLOW_HOP = AHEAD + 2
FAST_HOP = 2
TILE = 16
MESSAGE = STRIP + HALVES * TILE
POWER_STEPS = 6
LOW = 2.0 ** -1.875
SPAN = 2.0 ** 1.875 - LOW
MESH = pl.DeviceIdType.MESH


def encode(value, inverse):
    code = LOW + (SPAN * inverse) * jnp.abs(value)
    for _ in range(POWER_STEPS):
        code = code * code
    return jnp.where(value < 0, -code, code).astype(jnp.bfloat16)


def decode(code, scale):
    code = code.astype(jnp.float32)
    root = jnp.abs(code)
    for _ in range(POWER_STEPS):
        root = lax.rsqrt(root)
    value = (root - LOW) * (scale * (1 / SPAN))
    return jnp.where(code < 0, -value, value)


def halves_of(u):
    return HALVES if u == LAST else 1


def plan():
    todo = []

    def reduce(u, at):
        for stage, delay in enumerate((0, SLOW_HOP, SLOW_HOP + FAST_HOP, 2 * SLOW_HOP + FAST_HOP)):
            for h in range(halves_of(u)):
                todo.append((at + delay, 1 + stage, 1 + stage, (u, h)))

    for u in range(CHUNKS):
        for k in range(PER_CHUNK):
            todo.append((u, 0, 0, (u, k)))
        reduce(u, u + 1)
    for group, when in ((1, lambda p: p // 2 + 4), (2, lambda p: p + AHEAD + 1)):
        for p in range(PIECES):
            todo.append((when(p), 0, 0, (group * CHUNKS + p // PER_CHUNK, p % PER_CHUNK)))
        for j in range(CHUNKS):
            reduce(group * CHUNKS + j, when((j + 1) * PER_CHUNK - 1) + 1)
    return sorted(todo)


def kernel(n_cols, x_ref, hx_ref, out_ref, blocks, both, part, sib_in, snd, rcv, fin,
           load_sem, r1_send, r1_recv, r2_send, r2_recv, sib_send, sib_recv,
           z_send, z_recv, fin_send, fin_recv, out_sem):
    row = lax.axis_index("rows")
    col = lax.axis_index("cols")
    core = lax.rem(row, 2)
    z = row // 2
    upper = lax.rem(col, 2)
    edge = jnp.logical_or(z == 0, z == 3)
    inner = jnp.logical_or(z == 1, z == 2)
    sibling = (row + 1 - 2 * core, col)
    beside = (row + 2 - 4 * lax.rem(z, 2), col)
    across = ((3 - z) * 2 + core, col)
    half = (row, col + 1 - 2 * upper)

    def shifted(by):
        return (row, lax.rem(col + n_cols + by, n_cols))

    loads = [pltpu.make_async_copy(x_ref, both.at[:, pl.ds(0, BLOCK)], load_sem.at[0]),
             pltpu.make_async_copy(hx_ref, both.at[:, pl.ds(BLOCK, BLOCK)], load_sem.at[1])]
    for j in range(CHUNKS):
        loads.append(pltpu.make_async_copy(
            x_ref.at[:, pl.ds(j * STRIP, STRIP)], blocks.at[j], load_sem.at[2 + j]))

    barrier = pltpu.get_barrier_semaphore()
    for device in (sibling, beside, across, shifted(1), shifted(-1), shifted(2), shifted(-2)):
        pl.semaphore_signal(barrier, inc=1, device_id=device, device_id_type=MESH)
    pl.semaphore_wait(barrier, 7)

    def piece(slot, p):
        return blocks.at[slot + p // PER_CHUNK, pl.ds((p % PER_CHUNK) * PIECE, PIECE)]

    def own(p):
        return x_ref.at[pl.ds((p % PER_CHUNK) * PIECE, PIECE), pl.ds((p // PER_CHUNK) * STRIP, STRIP)]

    def remote(src, dst, send, recv, device):
        return pltpu.make_async_remote_copy(
            src_ref=src, dst_ref=dst, send_sem=send, recv_sem=recv,
            device_id=device, device_id_type=MESH)

    def two_back(p):
        return remote(own(p), piece(CHUNKS, p), r2_send.at[p], r2_recv.at[p], shifted(2))

    def one_back(p):
        if p < DIRECT:
            return remote(own(p), piece(2 * CHUNKS, p), r1_send.at[p], r1_recv.at[p], shifted(1))
        return remote(piece(upper * CHUNKS, p), piece(2 * CHUNKS, p), r1_send.at[p], r1_recv.at[p], half)

    def to_sibling(u):
        return remote(part.at[u, 1 - core], sib_in.at[u], sib_send.at[u], sib_recv.at[u], sibling)

    def message(buffer, s, u, h):
        size = STRIP // halves_of(u) + TILE
        return buffer.at[s, u, pl.ds(h * size, size)]

    def edge_to_inner(u, h):
        return remote(message(snd, 0, u, h), message(rcv, 0, u, h),
                      z_send.at[0, u, h], z_recv.at[0, u, h], beside)

    def inner_to_inner(u, h):
        return remote(message(snd, 0, u, h), message(rcv, 1, u, h),
                      z_send.at[0, u, h], z_recv.at[1, u, h], across)

    def inner_to_edge(u, h):
        return remote(message(snd, 1, u, h), message(rcv, 0, u, h),
                      z_send.at[1, u, h], z_recv.at[0, u, h], beside)

    def result(u, h):
        size = STRIP // halves_of(u)
        return (fin.at[u, pl.ds(h * size, size)],
                out_ref.at[core, ROUND_OF[u // CHUNKS], pl.ds((u % CHUNKS) * STRIP + h * size, size)])

    def fin_to_sibling(u, h):
        return remote(*result(u, h), fin_send.at[u, h], fin_recv.at[u, h], sibling)

    def fin_to_out(u, h):
        return pltpu.make_async_copy(*result(u, h), out_sem.at[u, h])

    def tile(start, i):
        return pl.ds(pl.multiple_of(start + i * TILE, TILE), TILE)

    def tiles_of(u):
        return STRIP // halves_of(u) // TILE

    def starts(u, h):
        return h * STRIP // halves_of(u), h * (STRIP // halves_of(u) + TILE)

    def write_code(s, u, h, value_of):
        at, to = starts(u, h)

        def scan(i, top):
            value = value_of(i)
            part[u, core, tile(at, i), :] = value
            return jnp.maximum(top, jnp.abs(value))
        top = lax.fori_loop(0, tiles_of(u), scan, jnp.full((TILE, BLOCK), 1e-30, jnp.float32))
        scale = (top * (1 + 2.0 ** -7)).astype(jnp.bfloat16)
        snd[s, u, tile(to, tiles_of(u)), :] = scale
        inverse = 1 / scale.astype(jnp.float32)

        @pl.loop(0, tiles_of(u))
        def _(i):
            snd[s, u, tile(to, i), :] = encode(part[u, core, tile(at, i), :], inverse)

    def reader(buffer, s, u, h):
        _, to = starts(u, h)
        scale = buffer[s, u, tile(to, tiles_of(u)), :].astype(jnp.float32)
        return lambda i: decode(buffer[s, u, tile(to, i), :], scale)

    def core_sum(u, h):
        at, _ = starts(u, h)
        return lambda i: part[u, core, tile(at, i), :] + sib_in[u, tile(at, i), :]

    waited = set()

    def once(kind, p, wait):
        if (kind, p) not in waited:
            waited.add((kind, p))
            wait()

    def wait_load(i):
        once("load", i, loads[i].wait)

    def wait_piece(group, p):
        once(group, p, (two_back(p) if group == 1 else one_back(p)).wait_recv)

    def multiply(u, k):
        wait_load(0)
        wait_load(1)
        if u < CHUNKS:
            wait_load(2 + u)
        else:
            wait_piece(u // CHUNKS, u % CHUNKS * PER_CHUNK + k)
        rows = pl.ds(k * PIECE, PIECE)
        got = lax.dot_general(
            blocks[u, rows, :], both[rows, :], (((0,), (0,)), ((), ())),
            preferred_element_type=jnp.float32)
        for kind in range(2):
            term = got[:, kind * BLOCK:(kind + 1) * BLOCK]
            part[u, kind] = term if k == 0 else part[u, kind] + term
        if k == PER_CHUNK - 1:
            to_sibling(u).start()

    def chip_sum(u, h):
        once("sibling", u, to_sibling(u).wait_recv)

        @pl.when(edge)
        def _():
            write_code(0, u, h, core_sum(u, h))
            edge_to_inner(u, h).start()

    def pair_sum(u, h):
        @pl.when(inner)
        def _():
            edge_to_inner(u, h).wait_recv()
            mine, theirs = core_sum(u, h), reader(rcv, 0, u, h)
            write_code(0, u, h, lambda i: mine(i) + theirs(i))
            inner_to_inner(u, h).start()

    def finish(u, h, buffer, s):
        at, _ = starts(u, h)
        read = reader(buffer, s, u, h)

        @pl.loop(0, tiles_of(u))
        def _(i):
            fin[u, tile(at, i), :] = read(i)
        fin_to_sibling(u, h).start()
        fin_to_out(u, h).start()

    def whole_sum(u, h):
        @pl.when(inner)
        def _():
            inner_to_inner(u, h).wait_recv()
            mine, theirs = reader(snd, 0, u, h), reader(rcv, 1, u, h)
            write_code(1, u, h, lambda i: mine(i) + theirs(i))
            inner_to_edge(u, h).start()
            finish(u, h, snd, 1)

    def edge_result(u, h):
        @pl.when(edge)
        def _():
            inner_to_edge(u, h).wait_recv()
            finish(u, h, rcv, 0)

    stage_of = (multiply, chip_sum, pair_sum, whole_sum, edge_result)
    todo = plan()
    sent_two = 0
    for p in range(PIECES):
        if p >= DIRECT:
            if p // PER_CHUNK < CHUNKS:
                wait_load(2 + p // PER_CHUNK)
            wait_piece(1, p)
        if p >= AHEAD:
            one_back(p - AHEAD).wait_send()
        one_back(p).start()
        while sent_two < min(PIECES, 2 * p + LEAD):
            two_back(sent_two).start()
            sent_two += 1
        if p == 0:
            for load in loads:
                load.start()
        while todo and todo[0][0] <= p:
            _, _, stage, args = todo.pop(0)
            stage_of[stage](*args)
    for _, _, stage, args in todo:
        stage_of[stage](*args)

    for p in range(PIECES - AHEAD, PIECES):
        one_back(p).wait_send()
    for p in range(PIECES):
        two_back(p).wait_send()
    for u in range(UNITS):
        to_sibling(u).wait_send()
        for h in range(halves_of(u)):
            fin_to_out(u, h).wait()
            fin_to_sibling(u, h).wait()

    @pl.when(edge)
    def _():
        for u in range(UNITS):
            for h in range(halves_of(u)):
                edge_to_inner(u, h).wait_send()

    @pl.when(inner)
    def _():
        for u in range(UNITS):
            for h in range(halves_of(u)):
                inner_to_inner(u, h).wait_send()
                inner_to_edge(u, h).wait_send()


def place(step):
    return step // 3, step % 3


def spread(in_ref, gram_ref, ham_ref):
    step = pl.program_id(0)

    @pl.when(step < 3)
    def _():
        gram_ref[0] = in_ref[0, 0].T

    @pl.when(step >= 3)
    def _():
        ham_ref[0] = in_ref[0, 0]


def per_device(n_cols, orbitals, applied):
    f32, bf16 = jnp.float32, jnp.bfloat16
    dma = pltpu.SemaphoreType.DMA
    sums = pl.pallas_call(
        functools.partial(kernel, n_cols),
        out_shape=jax.ShapeDtypeStruct((2, 3, BLOCK, BLOCK), f32),
        in_specs=[pl.BlockSpec(memory_space=pl.ANY)] * 2,
        out_specs=pl.BlockSpec(memory_space=pl.ANY),
        scratch_shapes=[
            pltpu.VMEM((3 * CHUNKS, GRID_ROWS, STRIP), bf16),
            pltpu.VMEM((GRID_ROWS, 2 * BLOCK), bf16),
            pltpu.VMEM((UNITS, 2, STRIP, BLOCK), f32),
            pltpu.VMEM((UNITS, STRIP, BLOCK), f32),
            pltpu.VMEM((2, UNITS, MESSAGE, BLOCK), bf16),
            pltpu.VMEM((2, UNITS, MESSAGE, BLOCK), bf16),
            pltpu.VMEM((UNITS, STRIP, BLOCK), f32),
            dma((2 + CHUNKS,)),
            dma((PIECES,)), dma((PIECES,)), dma((PIECES,)), dma((PIECES,)),
            dma((UNITS,)), dma((UNITS,)),
            dma((2, UNITS, HALVES)), dma((2, UNITS, HALVES)),
            dma((UNITS, HALVES)), dma((UNITS, HALVES)), dma((UNITS, HALVES)),
        ],
        compiler_params=pltpu.CompilerParams(
            collective_id=0, has_side_effects=True, vmem_limit_bytes=56 * 2**20),
    )(orbitals, applied)
    block = (1, BLOCK, BLOCK)
    gram, ham = pl.pallas_call(
        spread,
        grid=(6,),
        out_shape=[jax.ShapeDtypeStruct((3, BLOCK, BLOCK), f32)] * 2,
        in_specs=[pl.BlockSpec((1,) + block, lambda s: (s // 3, s % 3, 0, 0))],
        out_specs=[pl.BlockSpec(block, lambda s: (jnp.minimum(s, 2), 0, 0)),
                   pl.BlockSpec(block, lambda s: (jnp.maximum(s - 3, 0), 0, 0))],
    )(sums)
    return gram, ham


def solution(mesh):
    placed = (P("rows", "cols"), P("rows", "cols"))
    return jax.shard_map(
        functools.partial(per_device, mesh.shape["cols"]),
        mesh=mesh,
        in_specs=placed,
        out_specs=(P(None, "cols", None), P(None, "cols", None)),
        check_vma=False,
    )
```

time: 555 us -> 267 us (0.48)
  waiting for transfers between devices: 505 us -> 0 us
  Pallas kernels: 0 us -> 266 us
  matrix products: 17.5 us -> 0 us
  between operations: 14.1 us -> 0.64 us
  starting transfers between devices: 7.86 us -> 0 us
  local copies, waits for them, and re-layouts: 5.7 us -> 0 us
    ppermute x2 -> x0, waiting for transfers between devices: 358 us -> none  [from_behind(): return lax.ppermute(block, axis, route)]
    pallas_call x0 -> x2, Pallas kernels: none -> 266 us  [the longest x1 259 us: per_device(): pl.pallas_call(functools.partial(kernel, n_cols), out_shape=jax.ShapeDtyp...]
    psum x1 -> x0, waiting for transfers between devices: 147 us -> none  [per_device(): gram, ham = lax.psum((gram, ham), 'rows')]
    dot_general x6 -> x0, matrix products: 17.5 us -> none  [the longest x3 10.5 us: block_pair(): gram = jnp.dot(own.T, other, preferred_element_type=jnp.float32)]
    ppermute x2 -> x0, starting transfers between devices: 7.82 us -> none  [from_behind(): return lax.ppermute(block, axis, route)]
    unnamed x8 -> x0, local copies, waits for them, and re-layouts: 5.7 us -> none
  transfers between devices with their start and end apart: 3 -> 0, of which waited for: 3 -> 0; matrix products, arithmetic and copies ran while one was open for 2% -> 0% of each run, Pallas kernels for 0% -> 0%
where the time goes in v2:
time: 267 us
  Pallas kernels  266 us (100%)
    pallas_call x1, Pallas kernels, per_device(): pl.pallas_call(functools.partial(kernel, n_cols), out_shape=jax.ShapeDtyp...  259 us
    pallas_call x1, Pallas kernels, per_device(): pl.pallas_call(spread, grid=(6,), out_shape=[jax.ShapeDtypeStruct((3, BLO...  7.31 us

profile of v2, /device:TPU:1, one launch (start us, length us, event | category | flops | bytes accessed | tf_op | source)
XLA Modules:
  0.0 266.5 jit_solution(6037629021310100655)
XLA Ops:
  0.6 258.6 %shard_map.41.in_ref = f32[2,3,512,512]{3,2,1,0:T(8,128)} custom-call(bf16[4096,512]{1,0:T(8,128)(2,1)} %x_ref.1, bf16[4096,512]{1,0:T(8,128)(2,1)} %hx_ref.1), custom_call_target="tpu_custom_call" | custom-call | tf_op jit(solution)/shard_map/pallas_call | solution.py:323
  259.2 7.3 %shard_map.42 = (f32[3,512,512]{2,1,0:T(8,128)}, f32[3,512,512]{2,1,0:T(8,128)}) custom-call(f32[2,3,512,512]{3,2,1,0:T(8,128)} %shard_map.41.in_ref), custom_call_target="tpu_custom_call" | custom-call | tf_op jit(solution)/shard_map/pallas_call | solution.py:346

commit v3 on v2

--- a/solution.py
+++ b/solution.py
@@ -18,7 +18,7 @@
 UNITS = 3 * CHUNKS
 LAST = UNITS - 1
 HALVES = 2
-AHEAD = 4
+AHEAD = 5
 DIRECT = 4
 LEAD = 6
 SLOW_HOP = AHEAD + 2
@@ -60,14 +60,15 @@
                 todo.append((at + delay, 1 + stage, 1 + stage, (u, h)))
 
     for u in range(CHUNKS):
-        for k in range(PER_CHUNK):
-            todo.append((u, 0, 0, (u, k)))
+        todo.append((u, 0, 0, (u, 0, PER_CHUNK)))
         reduce(u, u + 1)
     for group, when in ((1, lambda p: p // 2 + 4), (2, lambda p: p + AHEAD + 1)):
-        for p in range(PIECES):
-            todo.append((when(p), 0, 0, (group * CHUNKS + p // PER_CHUNK, p % PER_CHUNK)))
         for j in range(CHUNKS):
-            reduce(group * CHUNKS + j, when((j + 1) * PER_CHUNK - 1) + 1)
+            u = group * CHUNKS + j
+            cuts = (0, PER_CHUNK - 2, PER_CHUNK) if u == LAST else (0, PER_CHUNK)
+            for start, stop in zip(cuts, cuts[1:]):
+                todo.append((when(j * PER_CHUNK + stop - 1), 0, 0, (u, start, stop)))
+            reduce(u, when((j + 1) * PER_CHUNK - 1) + 1)
     return sorted(todo)
 
 
@@ -196,21 +197,26 @@
     def wait_piece(group, p):
         once(group, p, (two_back(p) if group == 1 else one_back(p)).wait_recv)
 
-    def multiply(u, k):
+    def multiply(u, start, stop):
         wait_load(0)
         wait_load(1)
         if u < CHUNKS:
             wait_load(2 + u)
         else:
-            wait_piece(u // CHUNKS, u % CHUNKS * PER_CHUNK + k)
-        rows = pl.ds(k * PIECE, PIECE)
-        got = lax.dot_general(
-            blocks[u, rows, :], both[rows, :], (((0,), (0,)), ((), ())),
-            preferred_element_type=jnp.float32)
-        for kind in range(2):
-            term = got[:, kind * BLOCK:(kind + 1) * BLOCK]
-            part[u, kind] = term if k == 0 else part[u, kind] + term
-        if k == PER_CHUNK - 1:
+            for k in range(start, stop):
+                wait_piece(u // CHUNKS, u % CHUNKS * PER_CHUNK + k)
+        if start == 0:
+            part[u] = jnp.zeros((2, STRIP, BLOCK), jnp.float32)
+
+        @pl.loop(start, stop)
+        def _(k):
+            rows = pl.ds(pl.multiple_of(k * PIECE, PIECE), PIECE)
+            got = lax.dot_general(
+                blocks[u, rows, :], both[rows, :], (((0,), (0,)), ((), ())),
+                preferred_element_type=jnp.float32)
+            for kind in range(2):
+                part[u, kind] += got[:, kind * BLOCK:(kind + 1) * BLOCK]
+        if stop == PER_CHUNK:
             to_sibling(u).start()
 
     def chip_sum(u, h):
@@ -301,20 +307,20 @@
                 inner_to_edge(u, h).wait_send()
 
 
-def place(step):
-    return step // 3, step % 3
-
-
-def spread(in_ref, gram_ref, ham_ref):
-    step = pl.program_id(0)
-
-    @pl.when(step < 3)
-    def _():
-        gram_ref[0] = in_ref[0, 0].T
-
-    @pl.when(step >= 3)
-    def _():
-        ham_ref[0] = in_ref[0, 0]
+def spread(in_ref, gram_ref, ham_ref, before, after, in_sem, out_sem):
+    hams, ins, outs = [], [], []
+    for r in range(3):
+        ins.append(pltpu.make_async_copy(in_ref.at[0, r], before.at[r], in_sem.at[r]))
+        outs.append(pltpu.make_async_copy(after.at[r], gram_ref.at[r], out_sem.at[r]))
+        hams.append(pltpu.make_async_copy(in_ref.at[1, r], ham_ref.at[r], out_sem.at[3 + r]))
+    for copy in ins + hams:
+        copy.start()
+    for r in range(3):
+        ins[r].wait()
+        after[r] = before[r].T
+        outs[r].start()
+    for copy in hams + outs:
+        copy.wait()
 
 
 def per_device(n_cols, orbitals, applied):
@@ -342,14 +348,14 @@
         compiler_params=pltpu.CompilerParams(
             collective_id=0, has_side_effects=True, vmem_limit_bytes=56 * 2**20),
     )(orbitals, applied)
-    block = (1, BLOCK, BLOCK)
     gram, ham = pl.pallas_call(
         spread,
-        grid=(6,),
         out_shape=[jax.ShapeDtypeStruct((3, BLOCK, BLOCK), f32)] * 2,
-        in_specs=[pl.BlockSpec((1,) + block, lambda s: (s // 3, s % 3, 0, 0))],
-        out_specs=[pl.BlockSpec(block, lambda s: (jnp.minimum(s, 2), 0, 0)),
-                   pl.BlockSpec(block, lambda s: (jnp.maximum(s - 3, 0), 0, 0))],
+        in_specs=[pl.BlockSpec(memory_space=pl.ANY)],
+        out_specs=[pl.BlockSpec(memory_space=pl.ANY)] * 2,
+        scratch_shapes=[pltpu.VMEM((3, BLOCK, BLOCK), f32), pltpu.VMEM((3, BLOCK, BLOCK), f32),
+                        dma((3,)), dma((6,))],
+        compiler_params=pltpu.CompilerParams(vmem_limit_bytes=24 * 2**20),
     )(sums)
     return gram, ham
 

time: 267 us -> 263 us (0.985)
  Pallas kernels: 266 us -> 260 us
  local copies, waits for them, and re-layouts: 0 us -> 2.78 us
    pallas_call x1, Pallas kernels: 7.31 us -> 2.95 us  [per_device(): pl.pallas_call(spread, out_shape=[jax.ShapeDtypeStruct((3, BLOCK, BLOCK),...]
    unnamed x0 -> x2, local copies, waits for them, and re-layouts: none -> 2.78 us
where the time goes in v3:
time: 263 us
  Pallas kernels  260 us (99%)
  local copies, waits for them, and re-layouts  2.78 us (1%)
    pallas_call x1, Pallas kernels, per_device(): pl.pallas_call(functools.partial(kernel, n_cols), out_shape=jax.ShapeDtyp...  257 us

profile of v3, /device:TPU:1, one launch (start us, length us, event | category | flops | bytes accessed | tf_op | source)
XLA Modules:
  0.0 263.3 jit_solution(7753996694567833844)
XLA Ops:
  0.6 256.9 %shard_map.41.in_ref = f32[2,3,512,512]{3,2,1,0:T(8,128)} custom-call(bf16[4096,512]{1,0:T(8,128)(2,1)} %x_ref.1, bf16[4096,512]{1,0:T(8,128)(2,1)} %hx_ref.1), custom_call_target="tpu_custom_call" | custom-call | tf_op jit(solution)/shard_map/pallas_call | solution.py:329
  257.5 0.0 copy-start
  257.6 2.8 %copy-done = f32[2,3,512,512]{3,2,1,0:T(8,128)S(1)} copy-done((f32[2,3,512,512]{3,2,1,0:T(8,128)S(1)}, f32[2,3,512,512]{3,2,1,0:T(8,128)}, u32[]{:S(2)}) %copy-start) | copy-done | bytes 6291480
  260.3 3.0 %shard_map.42 = (f32[3,512,512]{2,1,0:T(8,128)}, f32[3,512,512]{2,1,0:T(8,128)}) custom-call(f32[2,3,512,512]{3,2,1,0:T(8,128)S(1)} %copy-done), custom_call_target="tpu_custom_call" | custom-call | tf_op jit(solution)/shard_map/pallas_call | solution.py:351
Async XLA Ops:
  257.5 2.8 %copy-start = (f32[2,3,512,512]{3,2,1,0:T(8,128)S(1)}, f32[2,3,512,512]{3,2,1,0:T(8,128)}, u32[]{:S(2)}) copy-start(f32[2,3,512,512]{3,2,1,0:T(8,128)} %shard_map.41.in_ref) | copy-start | bytes 18874372

commit v4 on v3

--- a/solution.py
+++ b/solution.py
@@ -21,7 +21,7 @@
 AHEAD = 5
 DIRECT = 4
 LEAD = 6
-SLOW_HOP = AHEAD + 2
+SLOW_HOP = AHEAD + 1
 FAST_HOP = 2
 TILE = 16
 MESSAGE = STRIP + HALVES * TILE

time: 263 us -> 262 us (level)
  Pallas kernels: 260 us -> 257 us
    pallas_call x1, Pallas kernels: 257 us -> 254 us  [per_device(): pl.pallas_call(functools.partial(kernel, n_cols), out_shape=jax.ShapeDtyp...]
where the time goes in v4:
time: 262 us; the launch traced here: 260 us
  Pallas kernels  257 us (98%)
  local copies, waits for them, and re-layouts  2.78 us (1%)
    pallas_call x1, Pallas kernels, per_device(): pl.pallas_call(functools.partial(kernel, n_cols), out_shape=jax.ShapeDtyp...  254 us

profile of v4, /device:TPU:1, one launch (start us, length us, event | category | flops | bytes accessed | tf_op | source)
XLA Modules:
  0.0 260.3 jit_solution(7937560643376834155)
XLA Ops:
  0.6 253.9 %shard_map.41.in_ref = f32[2,3,512,512]{3,2,1,0:T(8,128)} custom-call(bf16[4096,512]{1,0:T(8,128)(2,1)} %x_ref.1, bf16[4096,512]{1,0:T(8,128)(2,1)} %hx_ref.1), custom_call_target="tpu_custom_call" | custom-call | tf_op jit(solution)/shard_map/pallas_call | solution.py:329
  254.6 0.0 copy-start
  254.6 2.8 %copy-done = f32[2,3,512,512]{3,2,1,0:T(8,128)S(1)} copy-done((f32[2,3,512,512]{3,2,1,0:T(8,128)S(1)}, f32[2,3,512,512]{3,2,1,0:T(8,128)}, u32[]{:S(2)}) %copy-start) | copy-done | bytes 6291480
  257.3 3.0 %shard_map.42 = (f32[3,512,512]{2,1,0:T(8,128)}, f32[3,512,512]{2,1,0:T(8,128)}) custom-call(f32[2,3,512,512]{3,2,1,0:T(8,128)S(1)} %copy-done), custom_call_target="tpu_custom_call" | custom-call | tf_op jit(solution)/shard_map/pallas_call | solution.py:351
Async XLA Ops:
  254.6 2.8 %copy-start = (f32[2,3,512,512]{3,2,1,0:T(8,128)S(1)}, f32[2,3,512,512]{3,2,1,0:T(8,128)}, u32[]{:S(2)}) copy-start(f32[2,3,512,512]{3,2,1,0:T(8,128)} %shard_map.41.in_ref) | copy-start | bytes 18874372
